TPU v7x, 256 devices: a whole 4x4x8 slice. The times are simulated.
256 devices in a mesh: dp: 8 (over z), vocab: 32 (over y, x, core).
Axes of the slice: x: 4, y: 4, z: 8, core: 2. Of those that a mesh axis runs over, the one named last changes fastest.
Arguments:
- hidden: bfloat16 [3584, 2048], P('dp', 'vocab'), may hold values from -48 to 48
- head_weight: bfloat16 [2048, 77824], P(None, 'vocab'), may hold values from -4 to 4
- kept_tiles: int32 [3584, 32], P('dp'), may hold values from 0 to 607, all different within a row
- kept_count: int32 [3584], P('dp'), may hold values from 1 to 32
- teacher_probs: bfloat16 [3584, 32, 128], P('dp', 'vocab'), may hold values from 9.9658966e-05 to 0.0099487305
Outputs:
- distill_loss: float32 [], replicated
- grad_hidden: bfloat16 [3584, 2048], P('dp', 'vocab')
- grad_weight: bfloat16 [2048, 77824], P('dp', 'vocab')
Inputs may be any that keep to these rules, and one draw needn't show every extreme that they name: `kept_tiles`: the 32 entries of a row name different tiles.
All inputs are finite; a program needn't handle non-finite values.
Results may differ from a plain program's by a relative error of at most 0.018.
Values may be sent and summed in bfloat16 or wider, within the bound.
A program may use at most 128 MiB of HBM per device.

v0:
```python
import jax
import jax.numpy as jnp
from jax import lax
from jax.sharding import PartitionSpec as P

LOSS_SCALE = 1024.0


def shards(hidden, head_weight, kept_tiles, kept_count, teacher_probs):
    row_total = hidden.shape[0]
    shard_width = head_weight.shape[1]
    tile_width = teacher_probs.shape[2]
    tiles_here = shard_width // tile_width
    features = lax.all_gather(hidden, "vocab", axis=1, tiled=True)
    logits = jnp.dot(features, head_weight, preferred_element_type=jnp.float32)
    first_tile = lax.axis_index("vocab") * tiles_here
    tile_range = jnp.arange(tiles_here, dtype=jnp.int32)
    piece_probs = lax.all_gather(teacher_probs, "vocab", axis=1, tiled=True)
    target = jnp.zeros((row_total, shard_width), jnp.float32)
    width_slots = piece_probs.shape[1]
    slot_ids = jnp.arange(width_slots, dtype=jnp.int32)
    in_list = slot_ids[None, :] < kept_count[:, None]
    matches = ((kept_tiles - first_tile)[:, :, None] == tile_range[None, None, :]) & in_list[
        :, :, None
    ]
    placed = jnp.einsum(
        "rkn,rkc->rnc",
        matches.astype(jnp.bfloat16),
        piece_probs,
        preferred_element_type=jnp.float32,
    )
    target = placed.reshape(target.shape)
    probs_wide = piece_probs.astype(jnp.float32)
    values = probs_wide * in_list[:, :, None]
    mass_sum = jnp.sum(values, axis=(1, 2))
    weighted = jnp.sum(
        values * jnp.log(jnp.where(in_list[:, :, None], probs_wide, 1.0)), axis=(1, 2)
    )
    target, teacher_mass, weighted = (target, mass_sum, weighted)
    cross_local = jnp.sum(target * logits, axis=1)
    row_peak = lax.pmax(jnp.max(logits, axis=1), "vocab")
    local_mass = jnp.sum(jnp.exp(logits - row_peak[:, None]), axis=1)
    row_mass, cross_sum = lax.psum((local_mass, cross_local), "vocab")
    log_norm = row_peak + jnp.log(row_mass)
    divergence = (
        weighted / teacher_mass - jnp.log(teacher_mass) - cross_sum / teacher_mass + log_norm
    )
    replicas = lax.axis_size("dp")
    loss_sum = lax.psum(jnp.sum(divergence), "dp")
    distill_loss = loss_sum / (row_total * replicas)
    logit_grad = (
        LOSS_SCALE * (jnp.exp(logits - log_norm[:, None]) - target / teacher_mass[:, None])
    ).astype(jnp.bfloat16)
    hidden_cols = lax.psum_scatter(
        lax.dot_general(
            head_weight, logit_grad, (((1,), (1,)), ((), ())), preferred_element_type=jnp.float32
        ).astype(jnp.bfloat16),
        "vocab",
        scatter_dimension=0,
        tiled=True,
    ).astype(jnp.float32)
    grad_hidden = hidden_cols.T.astype(jnp.bfloat16)
    grad_weight = lax.psum_scatter(
        lax.dot_general(
            features, logit_grad, (((0,), (0,)), ((), ())), preferred_element_type=jnp.float32
        ).astype(jnp.bfloat16),
        "dp",
        scatter_dimension=0,
        tiled=True,
    )
    return (distill_loss, grad_hidden, grad_weight)


def solution(mesh):
    return jax.shard_map(
        shards,
        mesh=mesh,
        in_specs=(
            P("dp", "vocab"),
            P(None, "vocab"),
            P("dp", None),
            P("dp"),
            P("dp", "vocab", None),
        ),
        out_specs=(P(), P("dp", "vocab"), P("dp", "vocab")),
        check_vma=False,
    )
```

profile of v0, /device:TPU:73, one launch (start us, length us, event | category | flops | bytes accessed | tf_op | source)
XLA Modules:
  0.0 448.7 jit_solution(5048661621740002961)
XLA Ops:
  7.2 0.0 all-gather.5.cloned.1.call-start
  7.2 0.7 all-gather.5.cloned.1.call-update
  7.9 0.0 all-gather.3.cloned.1.call-start
  7.9 0.7 all-gather.3.cloned.1.call-update
  8.6 0.0 reduce-scatter.5.cloned.1.call-start
  8.7 0.7 fusion.12
  9.4 0.2 copy.20
  9.6 0.8 broadcast_subtract_fusion
  10.4 0.1 copy.19
  10.6 51.0 %all-gather.5.cloned.1.call-done = bf16[448,2048]{0,1:T(8,128)(2,1)} async-done(((bf16[448,64]{0,1:T(8,128)(2,1)}), bf16[448,2048]{0,1:T(8,128)(2,1)}) %all-gather.5.cloned.1.call-update) | async-done | bytes 1835024 | tf_op jit(solution)/shard_map/all_gather | solution.py:14
  61.6 11.5 %fusion.13 = (f32[448]{0:T(512)S(1)}, f32[448,2432]{1,0:T(8,128)}) fusion(bf16[448,2048]{0,1:T(8,128)(2,1)} %all-gather.5.cloned.1.call-done, bf16[2048,2432]{1,0:T(8,128)(2,1)} %param.6), kind=kOutput, calls=%fused_computation.24 | convolution fusion | flops 4463828480 | bytes 16156416 | tf_op jit(solution)/shard_map/dot_general | solution.py:15
  73.1 52.9 %pmax.7 = f32[448]{0:T(512)S(1)} all-reduce(f32[448]{0:T(512)S(1)} %get-tuple-element.22), channel_id=1, replica_groups=mesh['dp'=8,'vocab'=32] {'vocab'}, use_global_device_ids=true, to_apply=%region_5.6 | all-reduce | flops 448 | bytes 3584 | tf_op jit(solution)/shard_map/pmax | solution.py:41
  126.0 0.0 all-gather.3.cloned.1.call-done
  126.0 7.4 %fusion.6 = f32[448,19,128]{2,1,0:T(8,128)} fusion(bf16[448,32,128]{2,0,1:T(8,128)(2,1)} %all-gather.3.cloned.1.call-done, s32[448,32]{1,0:T(8,128)S(1)} %copy.19, pred[448,32]{1,0:T(8,128)(4,1)S(1)} %copy.20), kind=kOutput, calls=%fused_computation.10 | convolution fusion | flops 70275072 | bytes 8099840 | tf_op jit(solution)/shard_map/rkn,rkc->rnc/dot_general | solution.py:26
  133.4 6.1 %copy.22 = f32[448,19,128]{0,2,1:T(8,128)} copy(f32[448,19,128]{2,1,0:T(8,128)} %fusion.6) | data formatting | bytes 8716288 | tf_op jit(solution)/shard_map/rkn,rkc->rnc/dot_general | solution.py:26
  139.5 5.6 %copy.23 = f32[448,2432]{1,0:T(8,128)} copy(f32[448,2432]{0,1:T(8,128)} %bitcast.14) | data formatting | bytes 8716288 | tf_op jit(solution)/shard_map/reshape | solution.py:32
  145.1 4.6 %multiply_reduce_fusion = (f32[448]{0:T(512)S(1)}, f32[448]{0:T(512)S(1)}) fusion(f32[448,2432]{1,0:T(8,128)} %copy.23, f32[448,2432]{1,0:T(8,128)} %get-tuple-element.23, f32[448]{0:T(512)S(1)} %pmax.7), kind=kLoop, calls=%fused_computation.13 | loop fusion | flops 4357248 | bytes 8721664 | tf_op jit(solution)/shard_map/reduce_sum | solution.py:40
  149.7 57.7 %all-reduce = (f32[448]{0:T(512)S(1)}, f32[448]{0:T(512)S(1)}) all-reduce(f32[448]{0:T(512)S(1)} %get-tuple-element.13, f32[448]{0:T(512)S(1)} %get-tuple-element.12), channel_id=1, replica_groups=mesh['dp'=8,'vocab'=32] {'vocab'}, use_global_device_ids=true, to_apply=%region_7.8 | all-reduce | flops 896 | bytes 7168 | tf_op jit(solution)/shard_map/psum | solution.py:43
  207.5 8.8 %fusion.3 = (f32[448]{0:T(512)S(1)}, f32[448]{0:T(512)S(1)}) fusion(bf16[448,32,128]{2,0,1:T(8,128)(2,1)} %all-gather.3.cloned.1.call-done, f32[448,32]{0,1:T(8,128)S(1)} %get-tuple-element.20, pred[448,32]{0,1:T(8,128)(4,1)S(1)} %get-tuple-element.21), kind=kLoop, calls=%fused_computation.6 | loop fusion | flops 11009152 | bytes 3745280 | tf_op jit(solution)/shard_map/reduce_sum | solution.py:36
  216.3 0.6 add_reduce_fusion
  216.9 0.0 copy-start
  216.9 4.8 %multiply_convert_fusion = bf16[448,2432]{1,0:T(8,128)(2,1)S(1)} fusion(f32[448,2432]{1,0:T(8,128)} %copy.23, f32[448,2432]{1,0:T(8,128)} %get-tuple-element.23, f32[448]{0:T(512)S(1)} %get-tuple-element.15, f32[448]{0:T(512)S(1)} %get-tuple-element.19), kind=kLoop, calls=%fused_computation.11 | loop fusion | flops 5447680 | bytes 10898944 | tf_op jit(solution)/shard_map/convert_element_type | solution.py:53
  221.7 0.0 copy-done
  221.7 8.1 %fusion = bf16[2048,2432]{0,1:T(8,128)(2,1)} fusion(bf16[448,2432]{1,0:T(8,128)(2,1)S(1)} %multiply_convert_fusion, bf16[448,2048]{0,1:T(8,128)(2,1)S(1)} %copy-done), kind=kOutput, calls=%fused_computation.1 | convolution fusion | flops 4467720192 | bytes 13975552 | tf_op jit(solution)/shard_map/dot_general | solution.py:64
  229.8 0.0 reduce-scatter.5.cloned.1.call-update
  229.8 0.0 reduce-scatter.7.cloned.1.call-start
  229.8 11.1 %fusion.11 = bf16[2048,448]{0,1:T(8,128)(2,1)} fusion(bf16[448,2432]{1,0:T(8,128)(2,1)S(1)} %multiply_convert_fusion, bf16[2048,2432]{1,0:T(8,128)(2,1)} %param.6), kind=kOutput, calls=%fused_computation.18 | convolution fusion | flops 4463656960 | bytes 13975552 | tf_op jit(solution)/shard_map/dot_general | solution.py:55
  241.0 3.8 copy.27
  244.8 0.0 reduce-scatter.7.cloned.1.call-update
  244.8 12.2 %psum.23 = f32[]{:T(128)} all-reduce(f32[]{:T(128)} %get-tuple-element.18), channel_id=1, replica_groups=mesh['dp'=8,'vocab'=32] {'dp'}, use_global_device_ids=true, to_apply=%region_9.10 | all-reduce | flops 1 | bytes 8 | tf_op jit(solution)/shard_map/psum | solution.py:49
  257.6 94.5 %reduce-scatter.5.cloned.1.call-done = bf16[256,2432]{0,1:T(8,128)(2,1)} async-done(((bf16[2048,2432]{0,1:T(8,128)(2,1)}), bf16[256,2432]{0,1:T(8,128)(2,1)}) %reduce-scatter.5.cloned.1.call-update) | async-done | bytes 1245200 | tf_op jit(solution)/shard_map/reduce_scatter | solution.py:63
  352.1 2.4 copy.26
  354.5 86.5 %reduce-scatter.7.cloned.1.call-done = bf16[64,448]{1,0:T(8,128)(2,1)} async-done(((bf16[2048,448]{1,0:T(8,128)(2,1)}), bf16[64,448]{1,0:T(8,128)(2,1)}) %reduce-scatter.7.cloned.1.call-update) | async-done | bytes 57360
Async XLA Ops:
  7.2 54.4 %all-gather.5.cloned.1.call-start = ((), (), s32[]{:S(2)}) async-start(), calls=%async_computation.3 | async-start | bytes 2162688 | tf_op jit(solution)/shard_map/all_gather | solution.py:14
  7.9 118.1 %all-gather.3.cloned.1.call-start = ((), (), s32[]{:S(2)}) async-start(), calls=%async_computation.2 | async-start | bytes 3784704 | tf_op jit(solution)/shard_map/all_gather | solution.py:18
  8.6 343.5 %reduce-scatter.5.cloned.1.call-start = ((), (), s32[]{:S(2)}) async-start(), calls=%async_computation.4 | async-start | bytes 11206656 | tf_op jit(solution)/shard_map/reduce_scatter | solution.py:63
  216.9 4.8 %copy-start = (bf16[448,2048]{0,1:T(8,128)(2,1)S(1)}, bf16[448,2048]{0,1:T(8,128)(2,1)}, u32[]{:S(2)}) copy-start(bf16[448,2048]{0,1:T(8,128)(2,1)} %all-gather.5.cloned.1.call-done) | copy-start | bytes 5505028
  229.8 211.3 %reduce-scatter.7.cloned.1.call-start = ((), (), s32[]{:S(2)}) async-start(), calls=%async_computation.5 | async-start | bytes 2162688
Sparse Core Ops, SparseCore 0:
  10.6 50.9 all-gather.4
  64.1 49.8 all-gather.2
  229.9 122.1 reduce-scatter.4
  356.4 84.5 reduce-scatter.6
where the time goes:
time: 452 us; the launch traced here: 449 us
  waiting for transfers between devices  233 us (52%)
  blocking collectives  123 us (27%)
  matrix products  38.1 us (8%)
  other arithmetic  20.3 us (4%)
  local copies, waits for them, and re-layouts  18.2 us (4%)
  between operations  15.6 us (3%)
    reduce_scatter x1, waiting for transfers between devices, shards(): lax.psum_scatter(lax.dot_general(features, logit_grad, (((0,), (0,)), (()...  94.5 us
    unnamed x5, waiting for transfers between devices  87.9 us
    psum x1, blocking collectives, shards(): row_mass, cross_sum = lax.psum((local_mass, cross_local), 'vocab')  57.7 us
    pmax x1, blocking collectives, shards(): row_peak = lax.pmax(jnp.max(logits, axis=1), 'vocab')  52.9 us
    all_gather x1, waiting for transfers between devices, shards(): features = lax.all_gather(hidden, 'vocab', axis=1, tiled=True)  51 us
    psum x1, blocking collectives, shards(): loss_sum = lax.psum(jnp.sum(divergence), 'dp')  12.2 us
    dot_general x1, matrix products, shards(): logits = jnp.dot(features, head_weight, preferred_element_type=jnp.float32)  11.5 us
    dot_general x1, matrix products, shards(): lax.dot_general(head_weight, logit_grad, (((1,), (1,)), ((), ())), prefer...  11.1 us
  transfers between devices with their start and end apart: 4, of which 3 were waited for; matrix products, arithmetic and copies ran while one was open for 7% of the time, Pallas kernels for 0%

commit v1 on v0

v1 whole, which is shorter than its diff:
```python
import functools

import jax
import jax.numpy as jnp
from jax import lax
from jax.experimental import pallas as pl
from jax.experimental.pallas import tpu as pltpu
from jax.sharding import PartitionSpec as P

LOSS_SCALE = 1024.0
MESH = pl.DeviceIdType.MESH
NY, NX, NC = 4, 4, 2
NV = NY * NX * NC
NZ = 8
ROWS = 448
D = 2048
BLK = D // NV
TILE = 128
VOC = 2432
TILES = VOC // TILE
SLICE = D // NZ
STREAMS = 4
SUB = SLICE // STREAMS
RG = 16
COLS = ((0, 512), (512, 512), (1024, 512), (1536, 512), (2048, 384))
F32 = jnp.float32
BF16 = jnp.bfloat16


def mod(a, n):
    return lax.rem(a + n, n)


def to_all_lanes(rows4):
    flat = jnp.concatenate([rows4[a : a + 1, :] for a in range(4)], axis=1)
    return jnp.broadcast_to(flat, (TILE, 4 * TILE)).T[:ROWS, :]


def kernel(
    ht_ref, w_hbm, tiles_ref, count_ref, probs_ref,
    loss_ref, gh_ref, gw_ref,
    w_ref, hbuf, h_ref, pbuf, logit_ref, targ_ref, g_ref, z_ref, mass_ref, ln_ref,
    stat_out, stat_in, ghs, ghr, gwp, ring, l1, l2,
    w_sem, h1s, h1r, h2s, h2r, h3s, h3r, p1s, p1r, p2s, p2r, p3s, p3r,
    st_s, st_r, gh_s, gh_r, l1s, l1r, l2s, l2r, rs, rr,
):
    me = lax.axis_index("vocab")
    z = lax.axis_index("dp")
    c = lax.rem(me, NC)
    chip = lax.div(me, NC)
    x = lax.rem(chip, NX)
    y = lax.div(chip, NX)
    turn = 1 - 2 * c

    def at(yy, xx, cc):
        return {"vocab": (yy * NX + xx) * NC + cc}

    def rcopy(src, dst, ss, sr, dev):
        return pltpu.make_async_remote_copy(
            src_ref=src, dst_ref=dst, send_sem=ss, recv_sem=sr, device_id=dev, device_id_type=MESH
        )

    def got(ref, sem):
        rcopy(ref, ref, sem, sem, at(y, x, 1 - c)).wait_recv()

    def sent(ref, sem):
        rcopy(ref, ref, sem, sem, at(y, x, 1 - c)).wait_send()

    w_copy = pltpu.make_async_copy(w_hbm, w_ref, w_sem)
    w_copy.start()

    barrier = pltpu.get_barrier_semaphore()

    @pl.loop(1, NV)
    def _(d):
        pl.semaphore_signal(
            barrier, inc=1, device_id={"vocab": mod(me + d, NV)}, device_id_type=MESH
        )

    @pl.loop(1, NZ)
    def _(d):
        pl.semaphore_signal(barrier, inc=1, device_id={"dp": mod(z + d, NZ)}, device_id_type=MESH)

    hbuf[y, x, c] = ht_ref[...]
    pbuf[y, x, c] = probs_ref[...]
    pl.semaphore_wait(barrier, NV - 1 + NZ - 1)

    for d in range(1, 4):
        mine = hbuf.at[y, x, c]
        rcopy(mine, mine, h1s.at[d - 1], h1r.at[d - 1], at(y, mod(x + d, NX), c)).start()
    for d in range(1, 4):
        mine = pbuf.at[y, x, c]
        rcopy(mine, mine, p1s.at[d - 1], p1r.at[d - 1], at(mod(y + d, NY), x, c)).start()

    first = me * TILES
    local = tiles_ref[...] - first
    local = jnp.where((local >= 0) & (local < TILES), local, 32)
    listed = lax.broadcasted_iota(jnp.int32, (NV, ROWS), 0) < count_ref[...]
    local = jnp.where(listed, local, -1).astype(F32).astype(BF16)
    spread = (
        lax.shift_right_logical(lax.broadcasted_iota(jnp.int32, (NV, NV * RG), 1), 4)
        == lax.broadcasted_iota(jnp.int32, (NV, NV * RG), 0)
    )
    z_ref[...] = lax.dot_general(
        local, jnp.where(spread, 1.0, 0.0).astype(BF16), (((0,), (0,)), ((), ())),
        preferred_element_type=F32,
    )

    for d in range(1, 4):
        got(hbuf.at[y, mod(x - d, NX), c], h1r.at[d - 1])

    def hrow(yy):
        return hbuf.at[yy, :, c]

    def hrow_other(yy):
        return hbuf.at[yy, :, 1 - c]

    def pcol(xx):
        return pbuf.at[:, xx, c]

    def pcol_other(xx):
        return pbuf.at[:, xx, 1 - c]

    def hsend(yy, s, to):
        rcopy(hrow(yy), hrow(yy), h2s.at[s], h2r.at[s], at(to, x, c)).start()

    def hsib(yy, s):
        rcopy(hrow(yy), hrow(yy), h3s.at[s], h3r.at[s], at(y, x, 1 - c)).start()

    def psend(xx, s, to):
        rcopy(pcol(xx), pcol(xx), p2s.at[s], p2r.at[s], at(y, to, c)).start()

    def psib(xx, s):
        rcopy(pcol(xx), pcol(xx), p3s.at[s], p3r.at[s], at(y, x, 1 - c)).start()

    hsend(y, 0, mod(y + 1, NY))
    hsend(y, 1, mod(y - 1, NY))
    hsib(y, 0)

    for d in range(1, 4):
        got(pbuf.at[mod(y - d, NY), x, c], p1r.at[d - 1])
    psend(x, 0, mod(x + 1, NX))
    psend(x, 1, mod(x - 1, NX))
    psib(x, 0)

    y_from, y_to, y_far = mod(y - turn, NY), mod(y + turn, NY), mod(y + 2, NY)
    got(hrow(y_from), h2r.at[c])
    hsend(y_from, 2, y_to)
    hsib(y_from, 1)
    got(hrow(y_to), h2r.at[1 - c])
    hsib(y_to, 2)
    got(hrow(y_far), h2r.at[2])
    hsib(y_far, 3)
    got(hrow_other(y), h3r.at[0])
    got(hrow_other(y_to), h3r.at[1])
    got(hrow_other(y_from), h3r.at[2])
    got(hrow_other(y_far), h3r.at[3])

    for i in range(NV // 2):
        pair = hbuf[i // NX, i % NX].reshape(2 * BLK, ROWS)
        h_ref[:, i * 2 * BLK : (i + 1) * 2 * BLK] = pair.T
    w_copy.wait()

    x_from, x_to, x_far = mod(x - turn, NX), mod(x + turn, NX), mod(x + 2, NX)
    peak = jnp.full((ROWS, TILE), -jnp.inf, F32)
    for n, (lo, width) in enumerate(COLS):
        part = jnp.dot(h_ref[...], w_ref[:, lo : lo + width], preferred_element_type=F32)
        logit_ref[:, lo : lo + width] = part
        for t in range(width // TILE):
            peak = jnp.maximum(peak, part[:, t * TILE : (t + 1) * TILE])
        if n == 1:
            got(pcol(x_from), p2r.at[c])
            psend(x_from, 2, x_to)
            psib(x_from, 1)
            got(pcol(x_to), p2r.at[1 - c])
            psib(x_to, 2)
    peak = jnp.max(peak, axis=1, keepdims=True)
    mass = jnp.zeros((ROWS, TILE), F32)
    for t in range(TILES):
        mass = mass + jnp.exp(logit_ref[:, t * TILE : (t + 1) * TILE] - peak)
    mass = jnp.sum(mass, axis=1, keepdims=True)

    lane = lax.broadcasted_iota(jnp.int32, (ROWS, TILE), 1)
    packed = jnp.where(lane == 0, peak, jnp.where(lane == 1, mass, 0.0))
    packed = jnp.concatenate([packed, jnp.zeros((4 * TILE - ROWS, TILE), F32)], axis=0).T
    message = jnp.concatenate(
        [packed[i : i + 1, a * TILE : (a + 1) * TILE] for i in range(2) for a in range(4)], axis=0
    )
    stat_out[...] = message
    stat_in[me] = message

    @pl.loop(1, NV)
    def _(d):
        rcopy(stat_out, stat_in.at[me], st_s, st_r, {"vocab": mod(me + d, NV)}).start()

    got(pcol(x_far), p2r.at[2])
    psib(x_far, 3)
    got(pcol_other(x), p3r.at[0])
    got(pcol_other(x_to), p3r.at[1])
    got(pcol_other(x_from), p3r.at[2])
    got(pcol_other(x_far), p3r.at[3])

    own = lax.rem(lax.broadcasted_iota(jnp.int32, (RG, NV * RG), 1), RG) == (
        lax.broadcasted_iota(jnp.int32, (RG, NV * RG), 0)
    )

    @pl.loop(0, ROWS // RG)
    def _(g):
        rows = pl.ds(pl.multiple_of(g * RG, RG), RG)
        place = jnp.where(own, z_ref[rows, :], -1.0)
        blocks = [jnp.where(place == float(n), 1.0, 0.0).astype(BF16) for n in range(TILES)]
        blocks.append(jnp.where(place >= 0.0, 1.0, 0.0).astype(BF16))
        entries = pbuf[:, :, :, rows, :].reshape(NV * RG, TILE)
        placed = jnp.dot(jnp.concatenate(blocks, axis=0), entries, preferred_element_type=F32)
        for n in range(TILES):
            targ_ref[rows, n * TILE : (n + 1) * TILE] = placed[n * RG : (n + 1) * RG].astype(BF16)
        mass_ref[rows, :] = placed[TILES * RG :]

    teacher = jnp.sum(mass_ref[...], axis=1, keepdims=True)
    scale = 1.0 / teacher
    mass_ref[...] = jnp.broadcast_to(LOSS_SCALE * scale, (ROWS, TILE))
    cross = jnp.zeros((ROWS, TILE), F32)
    for t in range(TILES):
        cols = slice(t * TILE, (t + 1) * TILE)
        cross = cross + targ_ref[:, cols].astype(F32) * logit_ref[:, cols]
    entries = probs_ref[...].astype(F32)
    counts = jnp.broadcast_to(count_ref[...].astype(F32), (TILE, ROWS)).T
    weighted = jnp.where(counts > me.astype(F32), entries * jnp.log(entries), 0.0)
    shares = jnp.sum((weighted - cross) * scale)

    got(stat_in.at[pl.ds(0, NV - 1)], st_r)
    stats = stat_in[...]
    peaks, masses = stats[:, 0:4, :], stats[:, 4:8, :]
    top = jnp.max(peaks, axis=0)
    real = (
        lax.broadcasted_iota(jnp.int32, (4, TILE), 0) * TILE
        + lax.broadcasted_iota(jnp.int32, (4, TILE), 1)
    ) < ROWS
    total = jnp.where(real, jnp.sum(masses * jnp.exp(peaks - top[None]), axis=0), 1.0)
    log_norm = top + jnp.log(total)
    ln_ref[...] = to_all_lanes(log_norm)

    @pl.loop(0, TILES)
    def _(t):
        cols = pl.ds(pl.multiple_of(t * TILE, TILE), TILE)
        soft = LOSS_SCALE * jnp.exp(logit_ref[:, cols] - ln_ref[...])
        g_ref[:, cols] = (soft - targ_ref[:, cols].astype(F32) * mass_ref[...]).astype(BF16)

    def head_block(j):
        quarter = hbuf[lax.div(j, 2), pl.ds(2 * lax.rem(j, 2), 2)].reshape(SLICE, ROWS)
        for lo, width in COLS:
            gwp[j, :, lo : lo + width] = jnp.dot(
                quarter, g_ref[:, lo : lo + width], preferred_element_type=F32
            ).astype(BF16)

    def stream_rows(q):
        return pl.ds(q * SUB, SUB)

    def ahead(q):
        return 1 if q < STREAMS // 2 else -1

    def ring_send(q, src, step):
        rcopy(
            src, ring.at[q, step], rs.at[q, step], rr.at[q, step],
            {"dp": mod(z + ahead(q), NZ)},
        ).start()

    for way in (1, -1):
        j = mod(z - way, NZ)
        head_block(j)
        for q in range(STREAMS):
            if ahead(q) == way:
                ring_send(q, gwp.at[j, stream_rows(q)], 0)

    @pl.loop(0, 4)
    def _(i):
        rows = pl.ds(pl.multiple_of(i * 512, 512), 512)
        part = lax.dot_general(
            w_ref[rows, :], g_ref[...], (((1,), (1,)), ((), ())), preferred_element_type=F32
        )
        ghs[pl.ds(i * 8, 8)] = part.astype(BF16).reshape(8, BLK, ROWS)

    ghr[me] = ghs[me]

    @pl.loop(1, NV)
    def _(d):
        to = mod(me + d, NV)
        rcopy(ghs.at[to], ghr.at[me], gh_s, gh_r, {"vocab": to}).start()

    mass_col = jnp.log(teacher)
    common = jnp.sum(ln_ref[:, 0:1] - mass_col) * (1.0 / NV)
    l1[me] = jnp.broadcast_to(shares + common, (8, TILE))

    @pl.loop(1, NV)
    def _(d):
        rcopy(l1.at[me], l1.at[me], l1s, l1r, {"vocab": mod(me + d, NV)}).start()

    @pl.loop(2, NZ - 1)
    def _(i):
        head_block(mod(z + i, NZ))

    head_block(z)

    def ring_step(q, step):
        got(ring.at[q, step], rr.at[q, step])
        j = mod(z - ahead(q) * (2 + step) + NZ, NZ)
        both = ring[q, step].astype(F32) + gwp[j, q * SUB : (q + 1) * SUB, :].astype(F32)
        if step == NZ - 2:
            gw_ref[q * SUB : (q + 1) * SUB, :] = both.astype(BF16)
        else:
            ring[q, step] = both.astype(BF16)
            ring_send(q, ring.at[q, step], step + 1)

    order = (0, 2, 1, 3)
    for step in range(NZ - 1):
        for q in order:
            ring_step(q, step)
        if step == 1:
            got(l1.at[pl.ds(0, NV - 1)], l1r)
            l2[z] = jnp.sum(l1[...], axis=0)

            @pl.loop(1, NZ)
            def _(d):
                rcopy(l2.at[z], l2.at[z], l2s, l2r, {"dp": mod(z + d, NZ)}).start()

        if step == 3:
            got(ghr.at[pl.ds(0, NV - 1)], gh_r)
            total = jnp.zeros((BLK, ROWS), F32)
            for i in range(NV):
                total = total + ghr[i].astype(F32)
            gh_ref[...] = total.astype(BF16)
            got(l2.at[pl.ds(0, NZ - 1)], l2r)
            loss_ref[...] = jnp.sum(l2[...], axis=0) * (1.0 / (ROWS * NZ))

    for d in range(3):
        sent(hbuf.at[y, x, c], h1s.at[d])
        sent(pbuf.at[y, x, c], p1s.at[d])
        sent(hrow(y), h2s.at[d])
        sent(pcol(x), p2s.at[d])
    for d in range(4):
        sent(hrow(y), h3s.at[d])
        sent(pcol(x), p3s.at[d])
    sent(stat_in.at[pl.ds(0, NV - 1)], st_s)
    sent(ghr.at[pl.ds(0, NV - 1)], gh_s)
    sent(l1.at[pl.ds(0, NV - 1)], l1s)
    sent(l2.at[pl.ds(0, NZ - 1)], l2s)
    for q in range(STREAMS):
        for step in range(NZ - 1):
            sent(ring.at[q, step], rs.at[q, step])


def shards(hidden, head_weight, kept_tiles, kept_count, teacher_probs):
    vmem = pl.BlockSpec(memory_space=pltpu.VMEM)
    dma = pltpu.SemaphoreType.DMA
    loss, gh, gw = pl.pallas_call(
        kernel,
        out_shape=(
            jax.ShapeDtypeStruct((8, TILE), F32),
            jax.ShapeDtypeStruct((BLK, ROWS), BF16),
            jax.ShapeDtypeStruct((SLICE, VOC), BF16),
        ),
        in_specs=[vmem, pl.BlockSpec(memory_space=pl.ANY), vmem, vmem, vmem],
        out_specs=(vmem, vmem, vmem),
        scratch_shapes=[
            pltpu.VMEM((D, VOC), BF16),
            pltpu.VMEM((NY, NX, NC, BLK, ROWS), BF16),
            pltpu.VMEM((ROWS, D), BF16),
            pltpu.VMEM((NY, NX, NC, ROWS, TILE), BF16),
            pltpu.VMEM((ROWS, VOC), F32),
            pltpu.VMEM((ROWS, VOC), BF16),
            pltpu.VMEM((ROWS, VOC), BF16),
            pltpu.VMEM((ROWS, NV * RG), F32),
            pltpu.VMEM((ROWS, TILE), F32),
            pltpu.VMEM((ROWS, TILE), F32),
            pltpu.VMEM((8, TILE), F32),
            pltpu.VMEM((NV, 8, TILE), F32),
            pltpu.VMEM((NV, BLK, ROWS), BF16),
            pltpu.VMEM((NV, BLK, ROWS), BF16),
            pltpu.VMEM((NZ, SLICE, VOC), BF16),
            pltpu.VMEM((STREAMS, NZ - 1, SUB, VOC), BF16),
            pltpu.VMEM((NV, 8, TILE), F32),
            pltpu.VMEM((NZ, 8, TILE), F32),
            dma,
            dma((3,)), dma((3,)), dma((3,)), dma((3,)), dma((4,)), dma((4,)),
            dma((3,)), dma((3,)), dma((3,)), dma((3,)), dma((4,)), dma((4,)),
            dma, dma, dma, dma, dma, dma, dma, dma,
            dma((STREAMS, NZ - 1)), dma((STREAMS, NZ - 1)),
        ],
        compiler_params=pltpu.CompilerParams(
            collective_id=0, has_side_effects=True, vmem_limit_bytes=58 * 1024 * 1024
        ),
        cost_estimate=pl.CostEstimate(
            flops=6 * ROWS * D * VOC, bytes_accessed=2 * D * VOC, transcendentals=2 * ROWS * VOC
        ),
    )(
        hidden.T,
        head_weight,
        kept_tiles.T,
        kept_count.reshape(1, ROWS),
        teacher_probs.reshape(ROWS, TILE),
    )
    return loss[0, 0], gh.T, gw


def solution(mesh):
    return jax.shard_map(
        shards,
        mesh=mesh,
        in_specs=(
            P("dp", "vocab"),
            P(None, "vocab"),
            P("dp", None),
            P("dp"),
            P("dp", "vocab", None),
        ),
        out_specs=(P(), P("dp", "vocab"), P("dp", "vocab")),
        check_vma=False,
    )
```

time: 452 us -> 160 us (0.35)
  the two profiles are of different devices: /device:TPU:73 before, /device:TPU:1 now
where the time goes in v1:
time: 160 us
  Pallas kernels  154 us (96%)
  local copies, waits for them, and re-layouts  5.07 us (3%)
    pallas_call x1, Pallas kernels, shards(): pl.pallas_call(kernel, out_shape=(jax.ShapeDtypeStruct((8, TILE), F32), j...  154 us
    unnamed x2, local copies, waits for them, and re-layouts  3.89 us

profile of v1, /device:TPU:1, one launch (start us, length us, event | category | flops | bytes accessed | tf_op | source)
XLA Modules:
  0.0 159.7 jit_solution(12584539965360687462)
XLA Ops:
  0.6 154.0 %shard_map.76 = (f32[8,128]{1,0:T(8,128)}, bf16[64,448]{1,0:T(8,128)(2,1)}, bf16[256,2432]{1,0:T(8,128)(2,1)}) custom-call(bf16[64,448]{1,0:T(8,128)(2,1)} %bitcast.8, bf16[2048,2432]{1,0:T(8,128)(2,1)} %w_hbm.1, s32[32,448]{1,0:T(8,128)} %bitcast.9, s32[1,448]{1,0:T(1,128)} %bitcast.10, bf16[448,128]{1,0:T(8,128)(2,1)} %bitcast.7), custom_call_target="tpu_custom_call" | custom-call | flops 13388218368 | bytes 9961472 | tf_op jit(solution)/shard_map/pallas_call | solution.py:355
  154.6 1.2 slice.3
  155.8 1.5 copy.10
  157.3 2.4 %copy.11 = bf16[256,2432]{1,0:T(8,128)(2,1)} copy(bf16[256,2432]{1,0:T(8,128)(2,1)} %get-tuple-element.14) | data formatting | bytes 2490368

commit v2 on v0

v2 whole, which is shorter than its diff:
```python
import jax
import jax.numpy as jnp
from jax import lax
from jax.experimental import pallas as pl
from jax.experimental.pallas import tpu as pltpu
from jax.sharding import PartitionSpec as P

LOSS_SCALE = 1024.0
MESH = pl.DeviceIdType.MESH
NS = 4
NC = 2
NV = NS * NS * NC
NZ = 8
ROWS = 448
D = 2048
BLK = D // NV
TILE = 128
VOC = 2432
TILES = VOC // TILE
SLOTS = 3
WIDE = SLOTS * TILE
SLICE = D // NZ
RG = 16
COLS = ((0, 512), (512, 512), (1024, 512), (1536, 512), (2048, 384))
F32 = jnp.float32
BF16 = jnp.bfloat16


def mod(a, n):
    return lax.rem(a + n, n)


def flat_row(rows4):
    return jnp.concatenate([rows4[a : a + 1, :] for a in range(4)], axis=1)


def to_all_lanes(rows4):
    return jnp.broadcast_to(flat_row(rows4), (TILE, 4 * TILE)).T[:ROWS, :]


def tile_cols(t):
    return pl.ds(pl.multiple_of(t * TILE, TILE), TILE)


def kernel(
    ht_ref, w_hbm, tiles_ref, count_ref, probs_ref,
    loss_ref, gh_ref, gw_ref,
    w_ref, hall, h_ref, pbuf, logit_ref, targ_ref, g_ref, z_ref, mass_ref, ln_ref,
    wt_ref, t_in, grad_ref, gws, stat_out, stat_in, stat_z, ghs, ghr, l1, l2,
    w_sem, zhs, zhr, h_sems, p_sems, o_sems,
    st_s, st_r, gh_s, gh_r, l1s, l1r, l2s, l2r, sz_s, sz_r, ts, tr, ts2, tr2, ws, wr, ws2, wr2,
):
    me = lax.axis_index("vocab")
    z = lax.axis_index("dp")
    c = lax.rem(me, NC)
    chip = lax.div(me, NC)
    x = lax.rem(chip, NS)
    y = lax.div(chip, NS)
    a = x + c * (y - x)
    b = y + c * (x - y)

    def place(cc, bb, aa):
        yy = bb + cc * (aa - bb)
        xx = aa + cc * (bb - aa)
        return {"vocab": (yy * NS + xx) * NC + cc}

    sibling = {"vocab": chip * NC + 1 - c}

    def at_z(zz):
        return {"dp": zz}

    def owns3(zz):
        return lax.rem(zz, 3) == 0

    def tile_of(zz, s):
        return 16 + lax.div(zz, 3) if s == 2 else zz + 8 * s

    def rcopy(src, dst, ss, sr, dev):
        return pltpu.make_async_remote_copy(
            src_ref=src, dst_ref=dst, send_sem=ss, recv_sem=sr, device_id=dev, device_id_type=MESH
        )

    def got(ref, sem):
        rcopy(ref, ref, sem, sem, sibling).wait_recv()

    def sent(ref, sem):
        rcopy(ref, ref, sem, sem, sibling).wait_send()

    class Gather:
        def __init__(self, block, line, half, sems):
            self.block, self.line, self.half = block, line, half
            self.s, self.r = sems

        def first(self):
            for d in range(1, NS):
                ref = self.block(c, b, a)
                to = place(c, b, mod(a + d, NS))
                rcopy(ref, ref, self.s.at[d - 1], self.r.at[d - 1], to).start()

        def _side(self, bb, i):
            ref = self.line(c, bb)
            rcopy(ref, ref, self.s.at[7 + i], self.r.at[7 + i], sibling).start()

        def second(self):
            for d in range(1, NS):
                got(self.block(c, b, mod(a - d, NS)), self.r.at[d - 1])
            ref = self.line(c, b)
            for i, d in enumerate((1, -1)):
                rcopy(ref, ref, self.s.at[3 + i], self.r.at[3 + i], place(c, mod(b + d, NS), a)).start()
            self._side(b, 0)

        def relay(self):
            for i, d in enumerate((1, -1)):
                bb = mod(b - d, NS)
                got(self.line(c, bb), self.r.at[3 + i])
                ref = self.half(c, bb, i)
                rcopy(ref, ref, self.s.at[5 + i], self.r.at[5 + i], place(c, mod(b + d, NS), a)).start()
                self._side(bb, 1 + i)

        def last(self):
            bb = mod(b + 2, NS)
            for i in range(2):
                got(self.half(c, bb, i), self.r.at[5 + i])
            self._side(bb, 3)

        def finish(self):
            for i, d in enumerate((0, -1, 1, 2)):
                got(self.line(1 - c, mod(a + d, NS)), self.r.at[7 + i])

        def drain(self):
            for i in range(3):
                sent(self.block(c, b, a), self.s.at[i])
            for i in range(2):
                sent(self.line(c, b), self.s.at[3 + i])
                sent(self.half(c, b, i), self.s.at[5 + i])
            for i in range(4):
                sent(self.line(c, b), self.s.at[7 + i])

    own_h = Gather(
        lambda cc, bb, aa: hall.at[cc, bb, aa, 0],
        lambda cc, bb: hall.at[cc, bb, :, 0],
        lambda cc, bb, i: hall.at[cc, bb, pl.ds(2 * i, 2), 0],
        h_sems,
    )
    probs = Gather(
        lambda cc, bb, aa: pbuf.at[cc, bb, aa],
        lambda cc, bb: pbuf.at[cc, bb],
        lambda cc, bb, i: pbuf.at[cc, bb, pl.ds(2 * i, 2)],
        p_sems,
    )
    others = pl.ds(1, NZ - 1)
    other_h = Gather(
        lambda cc, bb, aa: hall.at[cc, bb, aa, others],
        lambda cc, bb: hall.at[cc, bb, :, others],
        lambda cc, bb, i: hall.at[cc, bb, pl.ds(2 * i, 2), others],
        o_sems,
    )

    w_copy = pltpu.make_async_copy(w_hbm, w_ref, w_sem)
    w_copy.start()

    barrier = pltpu.get_barrier_semaphore()

    @pl.loop(1, NV)
    def _(d):
        pl.semaphore_signal(
            barrier, inc=1, device_id={"vocab": mod(me + d, NV)}, device_id_type=MESH
        )

    @pl.loop(1, NZ)
    def _(d):
        pl.semaphore_signal(barrier, inc=1, device_id=at_z(mod(z + d, NZ)), device_id_type=MESH)

    hall[c, b, a, 0] = ht_ref[...]
    pbuf[c, b, a] = probs_ref[...]

    local = tiles_ref[...] - me * TILES
    local = jnp.where((local >= 0) & (local < TILES), local, 32)
    listed = lax.broadcasted_iota(jnp.int32, (NV, ROWS), 0) < count_ref[...]
    local = jnp.where(listed, local, -1).astype(F32).astype(BF16)
    slot = lax.shift_right_logical(lax.broadcasted_iota(jnp.int32, (NV, NV * RG), 1), 4)
    slot_b = lax.shift_right_logical(slot, 2) & 3
    slot_a = slot & 3
    position = jnp.where(slot < 16, slot_b * 8 + slot_a * 2, slot_a * 8 + slot_b * 2 + 1)
    spread = position == lax.broadcasted_iota(jnp.int32, (NV, NV * RG), 0)
    z_ref[...] = lax.dot_general(
        local, jnp.where(spread, 1.0, 0.0).astype(BF16), (((0,), (0,)), ((), ())),
        preferred_element_type=F32,
    )

    @pl.when(jnp.logical_not(owns3(z)))
    def _():
        for d in range(NZ):
            t_in[d, 2] = jnp.zeros((ROWS, TILE), BF16)

    pl.semaphore_wait(barrier, NV - 1 + NZ - 1)

    probs.first()
    own_h.first()
    for d in range(1, NZ):
        rcopy(
            hall.at[c, b, a, 0], hall.at[c, b, a, NZ - d], zhs.at[d - 1], zhr.at[d - 1],
            at_z(mod(z + d, NZ)),
        ).start()
    probs.second()
    own_h.second()

    w_copy.wait()
    for s in range(SLOTS):
        cols = tile_cols(tile_of(z, s))
        pieces = []
        for i in range(NV):
            cc, bb, aa = i // 16, i // 4 % 4, i % 4
            v = (bb * NS + aa) * NC if cc == 0 else (aa * NS + bb) * NC + 1
            pieces.append(w_ref[v * BLK : (v + 1) * BLK, cols])
        wt_ref[s * TILE : (s + 1) * TILE, :] = jnp.concatenate(pieces, axis=0).T

    probs.relay()
    own_h.relay()
    for d in range(1, NZ):
        got(hall.at[c, b, a, NZ - d], zhr.at[d - 1])
    other_h.first()
    probs.last()
    probs.finish()

    own = lax.rem(lax.broadcasted_iota(jnp.int32, (RG, NV * RG), 1), RG) == (
        lax.broadcasted_iota(jnp.int32, (RG, NV * RG), 0)
    )

    @pl.loop(0, ROWS // RG)
    def _(g):
        rows = pl.ds(pl.multiple_of(g * RG, RG), RG)
        spot = jnp.where(own, z_ref[rows, :], -1.0)
        blocks = [jnp.where(spot == float(n), 1.0, 0.0).astype(BF16) for n in range(TILES)]
        blocks.append(jnp.where(spot >= 0.0, 1.0, 0.0).astype(BF16))
        entries = pbuf[:, :, :, rows, :].reshape(NV * RG, TILE)
        placed = jnp.dot(jnp.concatenate(blocks, axis=0), entries, preferred_element_type=F32)
        for n in range(TILES):
            targ_ref[n, rows, :] = placed[n * RG : (n + 1) * RG].astype(BF16)
        mass_ref[rows, :] = placed[TILES * RG :]

    for d in range(1, NZ):
        to = mod(z + d, NZ)
        for s in range(2):
            rcopy(targ_ref.at[tile_of(to, s)], t_in.at[NZ - d, s], ts, tr, at_z(to)).start()

        @pl.when(owns3(to))
        def _():
            rcopy(targ_ref.at[tile_of(to, 2)], t_in.at[NZ - d, 2], ts2.at[d], tr2, at_z(to)).start()

    for s in range(2):
        t_in[0, s] = targ_ref[tile_of(z, s)]

    @pl.when(owns3(z))
    def _():
        t_in[0, 2] = targ_ref[tile_of(z, 2)]

    own_h.last()
    own_h.finish()
    other_h.second()
    for i in range(NV // 2):
        yy, xx = i // NS, i % NS
        pair = jnp.concatenate([hall[0, yy, xx, 0], hall[1, xx, yy, 0]], axis=0)
        h_ref[:, i * 2 * BLK : (i + 1) * 2 * BLK] = pair.T

    peak = jnp.full((ROWS, TILE), -jnp.inf, F32)
    for lo, width in COLS:
        part = jnp.dot(h_ref[...], w_ref[:, lo : lo + width], preferred_element_type=F32)
        for t in range(width // TILE):
            one = part[:, t * TILE : (t + 1) * TILE]
            logit_ref[lo // TILE + t] = one
            peak = jnp.maximum(peak, one)
    peak = jnp.max(peak, axis=1, keepdims=True)
    mass = jnp.zeros((ROWS, TILE), F32)
    for t in range(TILES):
        mass = mass + jnp.exp(logit_ref[t] - peak)
    mass = jnp.sum(mass, axis=1, keepdims=True)

    lane = lax.broadcasted_iota(jnp.int32, (ROWS, TILE), 1)

    def message_of(first, second):
        packed = jnp.where(lane == 0, first, jnp.where(lane == 1, second, 0.0))
        packed = jnp.concatenate([packed, jnp.zeros((4 * TILE - ROWS, TILE), F32)], axis=0).T
        return jnp.concatenate(
            [packed[i : i + 1, k * TILE : (k + 1) * TILE] for i in range(2) for k in range(4)],
            axis=0,
        )

    message = message_of(peak, mass)
    stat_out[...] = message
    stat_in[me] = message

    @pl.loop(1, NV)
    def _(d):
        rcopy(stat_out, stat_in.at[me], st_s, st_r, {"vocab": mod(me + d, NV)}).start()

    teacher = jnp.sum(mass_ref[...], axis=1, keepdims=True)
    scale = 1.0 / teacher
    mass_ref[...] = jnp.broadcast_to(LOSS_SCALE * scale, (ROWS, TILE))
    scale_rows = message_of(LOSS_SCALE * scale, jnp.log(teacher))
    cross = jnp.zeros((ROWS, TILE), F32)
    for t in range(TILES):
        cross = cross + targ_ref[t].astype(F32) * logit_ref[t]
    entries = probs_ref[...].astype(F32)
    counts = jnp.broadcast_to(count_ref[...].astype(F32), (TILE, ROWS)).T
    weighted = jnp.where(counts > me.astype(F32), entries * jnp.log(entries), 0.0)
    shares = jnp.sum((weighted - cross) * scale)

    got(stat_in.at[pl.ds(0, NV - 1)], st_r)
    stats = stat_in[...]
    peaks, masses = stats[:, 0:4, :], stats[:, 4:8, :]
    top = jnp.max(peaks, axis=0)
    real = (
        lax.broadcasted_iota(jnp.int32, (4, TILE), 0) * TILE
        + lax.broadcasted_iota(jnp.int32, (4, TILE), 1)
    ) < ROWS
    total = jnp.where(real, jnp.sum(masses * jnp.exp(peaks - top[None]), axis=0), 1.0)
    log_norm = jnp.where(real, top + jnp.log(total), 0.0)
    stat_z[0] = jnp.concatenate([log_norm, scale_rows[0:4]], axis=0)
    for d in range(1, NZ):
        rcopy(stat_z.at[0], stat_z.at[NZ - d], sz_s, sz_r, at_z(mod(z + d, NZ))).start()
    ln_ref[...] = to_all_lanes(log_norm)
    common = jnp.sum(jnp.where(real, log_norm - scale_rows[4:8], 0.0)) * (1.0 / NV)
    l1[me] = jnp.broadcast_to(shares + common, (8, TILE))

    @pl.loop(1, NV)
    def _(d):
        rcopy(l1.at[me], l1.at[me], l1s, l1r, {"vocab": mod(me + d, NV)}).start()

    @pl.loop(0, TILES)
    def _(t):
        soft = LOSS_SCALE * jnp.exp(logit_ref[t] - ln_ref[...])
        g_ref[:, tile_cols(t)] = (soft - targ_ref[t].astype(F32) * mass_ref[...]).astype(BF16)

    @pl.loop(0, 4)
    def _(i):
        rows = pl.ds(pl.multiple_of(i * 512, 512), 512)
        part = lax.dot_general(
            w_ref[rows, :], g_ref[...], (((1,), (1,)), ((), ())), preferred_element_type=F32
        )
        ghs[pl.ds(i * 8, 8)] = part.astype(BF16).reshape(8, BLK, ROWS)

    ghr[me] = ghs[me]

    other_h.relay()
    other_h.last()

    @pl.loop(1, NV)
    def _(d):
        to = mod(me + d, NV)
        rcopy(ghs.at[to], ghr.at[me], gh_s, gh_r, {"vocab": to}).start()

    got(l1.at[pl.ds(0, NV - 1)], l1r)
    l2[z] = jnp.sum(l1[...], axis=0)

    @pl.loop(1, NZ)
    def _(d):
        rcopy(l2.at[z], l2.at[z], l2s, l2r, at_z(mod(z + d, NZ))).start()

    got(stat_z.at[pl.ds(0, NZ - 1)], sz_r)
    other_h.finish()

    @pl.loop(0, NZ)
    def _(d):
        rows = hall[:, :, :, d].reshape(D, ROWS)
        part = jnp.dot(wt_ref[...], rows, preferred_element_type=F32)
        norm = flat_row(stat_z[d, 0:4])[:, :ROWS]
        soft = (LOSS_SCALE * jnp.exp(part - norm)).T
        for s in range(SLOTS):
            logit_ref[d * SLOTS + s] = soft[:, s * TILE : (s + 1) * TILE]

    got(t_in.at[pl.ds(1, NZ - 1), pl.ds(0, 2)], tr)

    @pl.when(owns3(z))
    def _():
        got(t_in.at[pl.ds(1, NZ - 1), 2], tr2)

    @pl.loop(0, NZ)
    def _(d):
        mass_ref[...] = to_all_lanes(stat_z[d, 4:8])
        for s in range(SLOTS):
            grad_ref[d, :, s * TILE : (s + 1) * TILE] = (
                logit_ref[d * SLOTS + s] - t_in[d, s].astype(F32) * mass_ref[...]
            ).astype(BF16)

    def head_block(j):
        yy, xx = lax.div(j, 2), 2 * lax.rem(j, 2)
        total = jnp.zeros((SLICE, WIDE), F32)
        for d in range(NZ):
            part = [
                hall[0, yy, xx, d], hall[1, xx, yy, d], hall[0, yy, xx + 1, d], hall[1, xx + 1, yy, d]
            ]
            total = total + jnp.dot(
                jnp.concatenate(part, axis=0), grad_ref[d], preferred_element_type=F32
            )
        return total.astype(BF16)

    @pl.loop(1, NZ)
    def _(i):
        j = mod(z + i, NZ)
        done = head_block(j)
        for s in range(SLOTS):
            gws[i, s] = done[:, s * TILE : (s + 1) * TILE]
        for s in range(2):
            rcopy(gws.at[i, s], gw_ref.at[:, tile_cols(tile_of(z, s))], ws, wr, at_z(j)).start()

        @pl.when(owns3(z))
        def _():
            rcopy(
                gws.at[i, 2], gw_ref.at[:, tile_cols(tile_of(z, 2))],
                ws2, wr2.at[lax.div(z, 3)], at_z(j),
            ).start()

    done = head_block(z)
    for s in range(2):
        gw_ref[:, tile_cols(tile_of(z, s))] = done[:, s * TILE : (s + 1) * TILE]

    @pl.when(owns3(z))
    def _():
        gw_ref[:, tile_cols(tile_of(z, 2))] = done[:, 2 * TILE :]

    got(ghr.at[pl.ds(0, NV - 1)], gh_r)
    sum_h = jnp.zeros((BLK, ROWS), F32)
    for i in range(NV):
        sum_h = sum_h + ghr[i].astype(F32)
    gh_ref[...] = sum_h.astype(BF16)
    got(l2.at[pl.ds(0, NZ - 1)], l2r)
    loss_ref[...] = jnp.sum(l2[...], axis=0) * (1.0 / (ROWS * NZ))

    probs.drain()
    own_h.drain()
    other_h.drain()
    for d in range(1, NZ):
        sent(hall.at[c, b, a, 0], zhs.at[d - 1])
    sent(stat_in.at[pl.ds(0, NV - 1)], st_s)
    sent(ghr.at[pl.ds(0, NV - 1)], gh_s)
    sent(l1.at[pl.ds(0, NV - 1)], l1s)
    sent(l2.at[pl.ds(0, NZ - 1)], l2s)
    sent(stat_z.at[pl.ds(0, NZ - 1)], sz_s)
    sent(t_in.at[pl.ds(1, NZ - 1), pl.ds(0, 2)], ts)
    for d in range(1, NZ):

        @pl.when(owns3(mod(z + d, NZ)))
        def _():
            sent(targ_ref.at[0], ts2.at[d])

    sent(gws.at[pl.ds(1, NZ - 1), pl.ds(0, 2)], ws)

    @pl.when(owns3(z))
    def _():
        sent(gws.at[pl.ds(1, NZ - 1), 2], ws2)

    got(gws.at[pl.ds(1, NZ - 1), pl.ds(0, 2)], wr)
    for i in range(SLOTS):

        @pl.when(z != 3 * i)
        def _():
            got(gws.at[0, 0], wr2.at[i])


def shards(hidden, head_weight, kept_tiles, kept_count, teacher_probs):
    vmem = pl.BlockSpec(memory_space=pltpu.VMEM)
    dma = pltpu.SemaphoreType.DMA
    loss, gh, gw = pl.pallas_call(
        kernel,
        out_shape=(
            jax.ShapeDtypeStruct((8, TILE), F32),
            jax.ShapeDtypeStruct((BLK, ROWS), BF16),
            jax.ShapeDtypeStruct((SLICE, VOC), BF16),
        ),
        in_specs=[vmem, pl.BlockSpec(memory_space=pl.ANY), vmem, vmem, vmem],
        out_specs=(vmem, vmem, vmem),
        scratch_shapes=[
            pltpu.VMEM((D, VOC), BF16),
            pltpu.VMEM((NC, NS, NS, NZ, BLK, ROWS), BF16),
            pltpu.VMEM((ROWS, D), BF16),
            pltpu.VMEM((NC, NS, NS, ROWS, TILE), BF16),
            pltpu.VMEM((NZ * SLOTS, ROWS, TILE), F32),
            pltpu.VMEM((TILES, ROWS, TILE), BF16),
            pltpu.VMEM((ROWS, VOC), BF16),
            pltpu.VMEM((ROWS, NV * RG), F32),
            pltpu.VMEM((ROWS, TILE), F32),
            pltpu.VMEM((ROWS, TILE), F32),
            pltpu.VMEM((WIDE, D), BF16),
            pltpu.VMEM((NZ, SLOTS, ROWS, TILE), BF16),
            pltpu.VMEM((NZ, ROWS, WIDE), BF16),
            pltpu.VMEM((NZ, SLOTS, SLICE, TILE), BF16),
            pltpu.VMEM((8, TILE), F32),
            pltpu.VMEM((NV, 8, TILE), F32),
            pltpu.VMEM((NZ, 8, TILE), F32),
            pltpu.VMEM((NV, BLK, ROWS), BF16),
            pltpu.VMEM((NV, BLK, ROWS), BF16),
            pltpu.VMEM((NV, 8, TILE), F32),
            pltpu.VMEM((NZ, 8, TILE), F32),
            dma, dma((NZ - 1,)), dma((NZ - 1,)),
            [dma((11,)), dma((11,))], [dma((11,)), dma((11,))], [dma((11,)), dma((11,))],
            dma, dma, dma, dma, dma, dma, dma, dma, dma, dma,
            dma, dma, dma((NZ,)), dma, dma, dma, dma, dma((SLOTS,)),
        ],
        compiler_params=pltpu.CompilerParams(
            collective_id=0, has_side_effects=True, vmem_limit_bytes=60 * 1024 * 1024
        ),
        cost_estimate=pl.CostEstimate(
            flops=8 * ROWS * D * VOC, bytes_accessed=2 * D * VOC, transcendentals=3 * ROWS * VOC
        ),
    )(
        hidden.T,
        head_weight,
        kept_tiles.T,
        kept_count.reshape(1, ROWS),
        teacher_probs.reshape(ROWS, TILE),
    )
    return loss[0, 0], gh.T, gw


def solution(mesh):
    return jax.shard_map(
        shards,
        mesh=mesh,
        in_specs=(
            P("dp", "vocab"),
            P(None, "vocab"),
            P("dp", None),
            P("dp"),
            P("dp", "vocab", None),
        ),
        out_specs=(P(), P("dp", "vocab"), P("dp", "vocab")),
        check_vma=False,
    )
```

time: 452 us -> 151 us (0.33)
  the two profiles are of different devices: /device:TPU:73 before, /device:TPU:29 now
where the time goes in v2:
time: 151 us
  Pallas kernels  146 us (97%)
  local copies, waits for them, and re-layouts  5.07 us (3%)
    pallas_call x1, Pallas kernels, shards(): pl.pallas_call(kernel, out_shape=(jax.ShapeDtypeStruct((8, TILE), F32), j...  146 us
    unnamed x2, local copies, waits for them, and re-layouts  3.89 us

profile of v2, /device:TPU:29, one launch (start us, length us, event | category | flops | bytes accessed | tf_op | source)
XLA Modules:
  0.0 151.2 jit_solution(15498948269178001560)
XLA Ops:
  0.6 145.5 %shard_map.76 = (f32[8,128]{1,0:T(8,128)}, bf16[64,448]{1,0:T(8,128)(2,1)}, bf16[256,2432]{1,0:T(8,128)(2,1)}) custom-call(bf16[64,448]{1,0:T(8,128)(2,1)} %bitcast.8, bf16[2048,2432]{1,0:T(8,128)(2,1)} %w_hbm.1, s32[32,448]{1,0:T(8,128)} %bitcast.9, s32[1,448]{1,0:T(1,128)} %bitcast.10, bf16[448,128]{1,0:T(8,128)(2,1)} %bitcast.7), custom_call_target="tpu_custom_call" | custom-call | flops 17850957824 | bytes 9961472 | tf_op jit(solution)/shard_map/pallas_call | solution.py:464
  146.2 1.2 slice.3
  147.4 1.5 copy.10
  148.8 2.4 %copy.11 = bf16[256,2432]{1,0:T(8,128)(2,1)} copy(bf16[256,2432]{1,0:T(8,128)(2,1)} %get-tuple-element.14) | data formatting | bytes 2490368

commit v3 on v2

--- a/solution.py
+++ b/solution.py
@@ -21,6 +21,10 @@
 WIDE = SLOTS * TILE
 SLICE = D // NZ
 RG = 16
+HALF = ROWS // 2
+ALL = ROWS * NZ
+KEPT = 3 * TILE
+STEP = 512
 COLS = ((0, 512), (512, 512), (1024, 512), (1536, 512), (2048, 384))
 F32 = jnp.float32
 BF16 = jnp.bfloat16
@@ -42,12 +46,18 @@
     return pl.ds(pl.multiple_of(t * TILE, TILE), TILE)
 
 
+def tile_rows(t):
+    return slice(t * ROWS, (t + 1) * ROWS) if isinstance(t, int) else pl.ds(
+        pl.multiple_of(t * ROWS, ROWS), ROWS
+    )
+
+
 def kernel(
     ht_ref, w_hbm, tiles_ref, count_ref, probs_ref,
     loss_ref, gh_ref, gw_ref,
-    w_ref, hall, h_ref, pbuf, logit_ref, targ_ref, g_ref, z_ref, mass_ref, ln_ref,
+    w_ref, hall, hown, zin, lnf_ref, col_ref, h_ref, pbuf, logit_ref, targ_ref, g_ref, z_ref, mass_ref, ln_ref,
     wt_ref, t_in, grad_ref, gws, stat_out, stat_in, stat_z, ghs, ghr, l1, l2,
-    w_sem, zhs, zhr, h_sems, p_sems, o_sems,
+    w_sem, zhs, zhr, h_sems, p_sems, q_sems, o_sems,
     st_s, st_r, gh_s, gh_r, l1s, l1r, l2s, l2r, sz_s, sz_r, ts, tr, ts2, tr2, ws, wr, ws2, wr2,
 ):
     me = lax.axis_index("vocab")
@@ -137,22 +147,26 @@
                 sent(self.line(c, b), self.s.at[7 + i])
 
     own_h = Gather(
-        lambda cc, bb, aa: hall.at[cc, bb, aa, 0],
-        lambda cc, bb: hall.at[cc, bb, :, 0],
-        lambda cc, bb, i: hall.at[cc, bb, pl.ds(2 * i, 2), 0],
+        lambda cc, bb, aa: hown.at[cc, bb, aa],
+        lambda cc, bb: hown.at[cc, bb],
+        lambda cc, bb, i: hown.at[cc, bb, pl.ds(2 * i, 2)],
         h_sems,
     )
-    probs = Gather(
-        lambda cc, bb, aa: pbuf.at[cc, bb, aa],
-        lambda cc, bb: pbuf.at[cc, bb],
-        lambda cc, bb, i: pbuf.at[cc, bb, pl.ds(2 * i, 2)],
-        p_sems,
-    )
-    others = pl.ds(1, NZ - 1)
+    def probs_gather(part, sems):
+        rows = pl.ds(part * HALF, HALF)
+        return Gather(
+            lambda cc, bb, aa: pbuf.at[cc, bb, aa, rows],
+            lambda cc, bb: pbuf.at[cc, bb, :, rows],
+            lambda cc, bb, i: pbuf.at[cc, bb, pl.ds(2 * i, 2), rows],
+            sems,
+        )
+
+    probs = [probs_gather(0, p_sems), probs_gather(1, q_sems)]
+    others = pl.ds(KEPT, ALL - KEPT)
     other_h = Gather(
-        lambda cc, bb, aa: hall.at[cc, bb, aa, others],
-        lambda cc, bb: hall.at[cc, bb, :, others],
-        lambda cc, bb, i: hall.at[cc, bb, pl.ds(2 * i, 2), others],
+        lambda cc, bb, aa: hall.at[cc, bb, aa, :, others],
+        lambda cc, bb: hall.at[cc, bb, :, :, others],
+        lambda cc, bb, i: hall.at[cc, bb, pl.ds(2 * i, 2), :, others],
         o_sems,
     )
 
@@ -171,7 +185,7 @@
     def _(d):
         pl.semaphore_signal(barrier, inc=1, device_id=at_z(mod(z + d, NZ)), device_id_type=MESH)
 
-    hall[c, b, a, 0] = ht_ref[...]
+    hown[c, b, a] = ht_ref[...]
     pbuf[c, b, a] = probs_ref[...]
 
     local = tiles_ref[...] - me * TILES
@@ -190,45 +204,29 @@
 
     @pl.when(jnp.logical_not(owns3(z)))
     def _():
-        for d in range(NZ):
-            t_in[d, 2] = jnp.zeros((ROWS, TILE), BF16)
+        t_in[2] = jnp.zeros((ALL, TILE), BF16)
 
     pl.semaphore_wait(barrier, NV - 1 + NZ - 1)
 
-    probs.first()
+    for one in probs:
+        one.first()
     own_h.first()
     for d in range(1, NZ):
         rcopy(
-            hall.at[c, b, a, 0], hall.at[c, b, a, NZ - d], zhs.at[d - 1], zhr.at[d - 1],
+            hown.at[c, b, a], zin.at[NZ - d], zhs.at[d - 1], zhr.at[d - 1],
             at_z(mod(z + d, NZ)),
         ).start()
-    probs.second()
+    for one in probs:
+        one.second()
     own_h.second()
-
-    w_copy.wait()
-    for s in range(SLOTS):
-        cols = tile_cols(tile_of(z, s))
-        pieces = []
-        for i in range(NV):
-            cc, bb, aa = i // 16, i // 4 % 4, i % 4
-            v = (bb * NS + aa) * NC if cc == 0 else (aa * NS + bb) * NC + 1
-            pieces.append(w_ref[v * BLK : (v + 1) * BLK, cols])
-        wt_ref[s * TILE : (s + 1) * TILE, :] = jnp.concatenate(pieces, axis=0).T
-
-    probs.relay()
-    own_h.relay()
-    for d in range(1, NZ):
-        got(hall.at[c, b, a, NZ - d], zhr.at[d - 1])
-    other_h.first()
-    probs.last()
-    probs.finish()
+    for one in probs:
+        one.relay()
 
     own = lax.rem(lax.broadcasted_iota(jnp.int32, (RG, NV * RG), 1), RG) == (
         lax.broadcasted_iota(jnp.int32, (RG, NV * RG), 0)
     )
 
-    @pl.loop(0, ROWS // RG)
-    def _(g):
+    def place_rows(g):
         rows = pl.ds(pl.multiple_of(g * RG, RG), RG)
         spot = jnp.where(own, z_ref[rows, :], -1.0)
         blocks = [jnp.where(spot == float(n), 1.0, 0.0).astype(BF16) for n in range(TILES)]
@@ -239,28 +237,48 @@
             targ_ref[n, rows, :] = placed[n * RG : (n + 1) * RG].astype(BF16)
         mass_ref[rows, :] = placed[TILES * RG :]
 
-    for d in range(1, NZ):
-        to = mod(z + d, NZ)
-        for s in range(2):
-            rcopy(targ_ref.at[tile_of(to, s)], t_in.at[NZ - d, s], ts, tr, at_z(to)).start()
-
-        @pl.when(owns3(to))
-        def _():
-            rcopy(targ_ref.at[tile_of(to, 2)], t_in.at[NZ - d, 2], ts2.at[d], tr2, at_z(to)).start()
+    for part in range(2):
+        probs[part].last()
+        probs[part].finish()
+        pl.loop(part * HALF // RG, (part + 1) * HALF // RG, unroll=2)(place_rows)
+        rows = pl.ds(part * HALF, HALF)
+        for d in range(1, NZ):
+            to = mod(z + d, NZ)
+            there = pl.ds((NZ - d) * ROWS + part * HALF, HALF)
+            for s in range(2):
+                rcopy(
+                    targ_ref.at[tile_of(to, s), rows], t_in.at[s, there], ts, tr, at_z(to)
+                ).start()
+
+            @pl.when(owns3(to))
+            def _():
+                rcopy(
+                    targ_ref.at[tile_of(to, 2), rows], t_in.at[2, there],
+                    ts2.at[d], tr2, at_z(to),
+                ).start()
+
+        if part == 0:
+            own_h.relay()
+            for d in range(1, NZ):
+                got(zin.at[NZ - d], zhr.at[d - 1])
+            parts = [hown[c, b, a]] + [zin[d] for d in range(1, NZ)]
+            hall[c, b, a] = jnp.concatenate(parts, axis=1)
+            other_h.first()
 
     for s in range(2):
-        t_in[0, s] = targ_ref[tile_of(z, s)]
+        t_in[s, 0:ROWS] = targ_ref[tile_of(z, s)]
 
     @pl.when(owns3(z))
     def _():
-        t_in[0, 2] = targ_ref[tile_of(z, 2)]
+        t_in[2, 0:ROWS] = targ_ref[tile_of(z, 2)]
 
     own_h.last()
     own_h.finish()
     other_h.second()
+    w_copy.wait()
     for i in range(NV // 2):
         yy, xx = i // NS, i % NS
-        pair = jnp.concatenate([hall[0, yy, xx, 0], hall[1, xx, yy, 0]], axis=0)
+        pair = jnp.concatenate([hown[0, yy, xx], hown[1, xx, yy]], axis=0)
         h_ref[:, i * 2 * BLK : (i + 1) * 2 * BLK] = pair.T
 
     peak = jnp.full((ROWS, TILE), -jnp.inf, F32)
@@ -268,12 +286,12 @@
         part = jnp.dot(h_ref[...], w_ref[:, lo : lo + width], preferred_element_type=F32)
         for t in range(width // TILE):
             one = part[:, t * TILE : (t + 1) * TILE]
-            logit_ref[lo // TILE + t] = one
+            logit_ref[tile_rows(lo // TILE + t), :] = one
             peak = jnp.maximum(peak, one)
     peak = jnp.max(peak, axis=1, keepdims=True)
     mass = jnp.zeros((ROWS, TILE), F32)
     for t in range(TILES):
-        mass = mass + jnp.exp(logit_ref[t] - peak)
+        mass = mass + jnp.exp(logit_ref[tile_rows(t), :] - peak)
     mass = jnp.sum(mass, axis=1, keepdims=True)
 
     lane = lax.broadcasted_iota(jnp.int32, (ROWS, TILE), 1)
@@ -294,13 +312,22 @@
     def _(d):
         rcopy(stat_out, stat_in.at[me], st_s, st_r, {"vocab": mod(me + d, NV)}).start()
 
+    for s in range(SLOTS):
+        cols = tile_cols(tile_of(z, s))
+        pieces = []
+        for i in range(NV):
+            cc, bb, aa = i // 16, i // 4 % 4, i % 4
+            v = (bb * NS + aa) * NC if cc == 0 else (aa * NS + bb) * NC + 1
+            pieces.append(w_ref[v * BLK : (v + 1) * BLK, cols])
+        wt_ref[s * TILE : (s + 1) * TILE, :] = jnp.concatenate(pieces, axis=0).T
+
     teacher = jnp.sum(mass_ref[...], axis=1, keepdims=True)
     scale = 1.0 / teacher
     mass_ref[...] = jnp.broadcast_to(LOSS_SCALE * scale, (ROWS, TILE))
     scale_rows = message_of(LOSS_SCALE * scale, jnp.log(teacher))
     cross = jnp.zeros((ROWS, TILE), F32)
     for t in range(TILES):
-        cross = cross + targ_ref[t].astype(F32) * logit_ref[t]
+        cross = cross + targ_ref[t].astype(F32) * logit_ref[tile_rows(t), :]
     entries = probs_ref[...].astype(F32)
     counts = jnp.broadcast_to(count_ref[...].astype(F32), (TILE, ROWS)).T
     weighted = jnp.where(counts > me.astype(F32), entries * jnp.log(entries), 0.0)
@@ -329,7 +356,7 @@
 
     @pl.loop(0, TILES)
     def _(t):
-        soft = LOSS_SCALE * jnp.exp(logit_ref[t] - ln_ref[...])
+        soft = LOSS_SCALE * jnp.exp(logit_ref[tile_rows(t), :] - ln_ref[...])
         g_ref[:, tile_cols(t)] = (soft - targ_ref[t].astype(F32) * mass_ref[...]).astype(BF16)
 
     @pl.loop(0, 4)
@@ -341,6 +368,7 @@
         ghs[pl.ds(i * 8, 8)] = part.astype(BF16).reshape(8, BLK, ROWS)
 
     ghr[me] = ghs[me]
+    hall[:, :, :, :, 0:KEPT] = hown[:, :, :, :, 0:KEPT]
 
     other_h.relay()
     other_h.last()
@@ -358,40 +386,50 @@
         rcopy(l2.at[z], l2.at[z], l2s, l2r, at_z(mod(z + d, NZ))).start()
 
     got(stat_z.at[pl.ds(0, NZ - 1)], sz_r)
+    lnf_ref[...] = jnp.concatenate(
+        [flat_row(stat_z[d, 0:4])[:, :ROWS] for d in range(NZ)], axis=1
+    )
+    for d in range(NZ):
+        col_ref[d * ROWS : (d + 1) * ROWS, :] = to_all_lanes(stat_z[d, 4:8])
     other_h.finish()
 
-    @pl.loop(0, NZ)
-    def _(d):
-        rows = hall[:, :, :, d].reshape(D, ROWS)
+    @pl.loop(0, ALL // STEP)
+    def _(k):
+        lanes = pl.ds(pl.multiple_of(k * STEP, STEP), STEP)
+        rows = hall[:, :, :, :, lanes].reshape(D, STEP)
         part = jnp.dot(wt_ref[...], rows, preferred_element_type=F32)
-        norm = flat_row(stat_z[d, 0:4])[:, :ROWS]
-        soft = (LOSS_SCALE * jnp.exp(part - norm)).T
+        soft = (LOSS_SCALE * jnp.exp(part - lnf_ref[:, lanes])).T
         for s in range(SLOTS):
-            logit_ref[d * SLOTS + s] = soft[:, s * TILE : (s + 1) * TILE]
-
-    got(t_in.at[pl.ds(1, NZ - 1), pl.ds(0, 2)], tr)
+            logit_ref[pl.ds(pl.multiple_of(s * ALL + k * STEP, STEP), STEP), :] = (
+                soft[:, s * TILE : (s + 1) * TILE]
+            )
+
+    got(t_in.at[pl.ds(0, 2), pl.ds(ROWS, ALL - ROWS)], tr)
 
     @pl.when(owns3(z))
     def _():
-        got(t_in.at[pl.ds(1, NZ - 1), 2], tr2)
-
-    @pl.loop(0, NZ)
-    def _(d):
-        mass_ref[...] = to_all_lanes(stat_z[d, 4:8])
+        got(t_in.at[2, pl.ds(ROWS, ALL - ROWS)], tr2)
+
+    @pl.loop(0, ALL // STEP)
+    def _(k):
+        rows = pl.ds(pl.multiple_of(k * STEP, STEP), STEP)
         for s in range(SLOTS):
-            grad_ref[d, :, s * TILE : (s + 1) * TILE] = (
-                logit_ref[d * SLOTS + s] - t_in[d, s].astype(F32) * mass_ref[...]
+            soft = logit_ref[pl.ds(pl.multiple_of(s * ALL + k * STEP, STEP), STEP), :]
+            grad_ref[rows, s * TILE : (s + 1) * TILE] = (
+                soft - t_in[s, rows, :].astype(F32) * col_ref[rows, :]
             ).astype(BF16)
 
     def head_block(j):
         yy, xx = lax.div(j, 2), 2 * lax.rem(j, 2)
         total = jnp.zeros((SLICE, WIDE), F32)
-        for d in range(NZ):
+        for k in range(ALL // STEP):
+            lanes = slice(k * STEP, (k + 1) * STEP)
             part = [
-                hall[0, yy, xx, d], hall[1, xx, yy, d], hall[0, yy, xx + 1, d], hall[1, xx + 1, yy, d]
+                hall[0, yy, xx, :, lanes], hall[1, xx, yy, :, lanes],
+                hall[0, yy, xx + 1, :, lanes], hall[1, xx + 1, yy, :, lanes],
             ]
             total = total + jnp.dot(
-                jnp.concatenate(part, axis=0), grad_ref[d], preferred_element_type=F32
+                jnp.concatenate(part, axis=0), grad_ref[lanes, :], preferred_element_type=F32
             )
         return total.astype(BF16)
 
@@ -427,17 +465,18 @@
     got(l2.at[pl.ds(0, NZ - 1)], l2r)
     loss_ref[...] = jnp.sum(l2[...], axis=0) * (1.0 / (ROWS * NZ))
 
-    probs.drain()
+    for one in probs:
+        one.drain()
     own_h.drain()
     other_h.drain()
     for d in range(1, NZ):
-        sent(hall.at[c, b, a, 0], zhs.at[d - 1])
+        sent(hown.at[c, b, a], zhs.at[d - 1])
     sent(stat_in.at[pl.ds(0, NV - 1)], st_s)
     sent(ghr.at[pl.ds(0, NV - 1)], gh_s)
     sent(l1.at[pl.ds(0, NV - 1)], l1s)
     sent(l2.at[pl.ds(0, NZ - 1)], l2s)
     sent(stat_z.at[pl.ds(0, NZ - 1)], sz_s)
-    sent(t_in.at[pl.ds(1, NZ - 1), pl.ds(0, 2)], ts)
+    sent(t_in.at[pl.ds(0, 2), pl.ds(ROWS, ALL - ROWS)], ts)
     for d in range(1, NZ):
 
         @pl.when(owns3(mod(z + d, NZ)))
@@ -472,18 +511,22 @@
         out_specs=(vmem, vmem, vmem),
         scratch_shapes=[
             pltpu.VMEM((D, VOC), BF16),
-            pltpu.VMEM((NC, NS, NS, NZ, BLK, ROWS), BF16),
+            pltpu.VMEM((NC, NS, NS, BLK, ALL), BF16),
+            pltpu.VMEM((NC, NS, NS, BLK, ROWS), BF16),
+            pltpu.VMEM((NZ, BLK, ROWS), BF16),
+            pltpu.VMEM((1, ALL), F32),
+            pltpu.VMEM((ALL, TILE), F32),
             pltpu.VMEM((ROWS, D), BF16),
             pltpu.VMEM((NC, NS, NS, ROWS, TILE), BF16),
-            pltpu.VMEM((NZ * SLOTS, ROWS, TILE), F32),
+            pltpu.VMEM((SLOTS * ALL, TILE), F32),
             pltpu.VMEM((TILES, ROWS, TILE), BF16),
             pltpu.VMEM((ROWS, VOC), BF16),
             pltpu.VMEM((ROWS, NV * RG), F32),
             pltpu.VMEM((ROWS, TILE), F32),
             pltpu.VMEM((ROWS, TILE), F32),
             pltpu.VMEM((WIDE, D), BF16),
-            pltpu.VMEM((NZ, SLOTS, ROWS, TILE), BF16),
-            pltpu.VMEM((NZ, ROWS, WIDE), BF16),
+            pltpu.VMEM((SLOTS, ALL, TILE), BF16),
+            pltpu.VMEM((ALL, WIDE), BF16),
             pltpu.VMEM((NZ, SLOTS, SLICE, TILE), BF16),
             pltpu.VMEM((8, TILE), F32),
             pltpu.VMEM((NV, 8, TILE), F32),
@@ -493,7 +536,7 @@
             pltpu.VMEM((NV, 8, TILE), F32),
             pltpu.VMEM((NZ, 8, TILE), F32),
             dma, dma((NZ - 1,)), dma((NZ - 1,)),
-            [dma((11,)), dma((11,))], [dma((11,)), dma((11,))], [dma((11,)), dma((11,))],
+            [dma((11,)), dma((11,))], [dma((11,)), dma((11,))], [dma((11,)), dma((11,))], [dma((11,)), dma((11,))],
             dma, dma, dma, dma, dma, dma, dma, dma, dma, dma,
             dma, dma, dma((NZ,)), dma, dma, dma, dma, dma((SLOTS,)),
         ],

time: 151 us -> 141 us (0.934)
  the two profiles are of different devices: /device:TPU:29 before, /device:TPU:1 now
where the time goes in v3:
time: 141 us
  Pallas kernels  135 us (96%)
  local copies, waits for them, and re-layouts  5.07 us (4%)
    pallas_call x1, Pallas kernels, shards(): pl.pallas_call(kernel, out_shape=(jax.ShapeDtypeStruct((8, TILE), F32), j...  135 us
    unnamed x2, local copies, waits for them, and re-layouts  3.89 us

profile of v3, /device:TPU:1, one launch (start us, length us, event | category | flops | bytes accessed | tf_op | source)
XLA Modules:
  0.0 141.1 jit_solution(11286188470867476255)
XLA Ops:
  0.6 135.3 %shard_map.76 = (f32[8,128]{1,0:T(8,128)}, bf16[64,448]{1,0:T(8,128)(2,1)}, bf16[256,2432]{1,0:T(8,128)(2,1)}) custom-call(bf16[64,448]{1,0:T(8,128)(2,1)} %bitcast.8, bf16[2048,2432]{1,0:T(8,128)(2,1)} %w_hbm.1, s32[32,448]{1,0:T(8,128)} %bitcast.9, s32[1,448]{1,0:T(1,128)} %bitcast.10, bf16[448,128]{1,0:T(8,128)(2,1)} %bitcast.7), custom_call_target="tpu_custom_call" | custom-call | flops 17850957824 | bytes 9961472 | tf_op jit(solution)/shard_map/pallas_call | solution.py:503
  136.0 1.2 slice.3
  137.2 1.5 %copy.10 = bf16[448,64]{0,1:T(8,128)(2,1)} copy(bf16[448,64]{0,1:T(8,128)(2,1)} %bitcast.6) | data formatting | bytes 114688
  138.6 2.4 %copy.11 = bf16[256,2432]{1,0:T(8,128)(2,1)} copy(bf16[256,2432]{1,0:T(8,128)(2,1)} %get-tuple-element.14) | data formatting | bytes 2490368

commit v4 on v3

--- a/solution.py
+++ b/solution.py
@@ -21,7 +21,7 @@
 WIDE = SLOTS * TILE
 SLICE = D // NZ
 RG = 16
-HALF = ROWS // 2
+PARTS = ((0, 96), (96, 160), (256, 192))
 ALL = ROWS * NZ
 KEPT = 3 * TILE
 STEP = 512
@@ -57,7 +57,7 @@
     loss_ref, gh_ref, gw_ref,
     w_ref, hall, hown, zin, lnf_ref, col_ref, h_ref, pbuf, logit_ref, targ_ref, g_ref, z_ref, mass_ref, ln_ref,
     wt_ref, t_in, grad_ref, gws, stat_out, stat_in, stat_z, ghs, ghr, l1, l2,
-    w_sem, zhs, zhr, h_sems, p_sems, q_sems, o_sems,
+    w_sem, zhs, zhr, h_sems, p_sems, q_sems, v_sems, o_sems,
     st_s, st_r, gh_s, gh_r, l1s, l1r, l2s, l2r, sz_s, sz_r, ts, tr, ts2, tr2, ws, wr, ws2, wr2,
 ):
     me = lax.axis_index("vocab")
@@ -153,7 +153,7 @@
         h_sems,
     )
     def probs_gather(part, sems):
-        rows = pl.ds(part * HALF, HALF)
+        rows = pl.ds(*PARTS[part])
         return Gather(
             lambda cc, bb, aa: pbuf.at[cc, bb, aa, rows],
             lambda cc, bb: pbuf.at[cc, bb, :, rows],
@@ -161,7 +161,7 @@
             sems,
         )
 
-    probs = [probs_gather(0, p_sems), probs_gather(1, q_sems)]
+    probs = [probs_gather(i, sems) for i, sems in enumerate((p_sems, q_sems, v_sems))]
     others = pl.ds(KEPT, ALL - KEPT)
     other_h = Gather(
         lambda cc, bb, aa: hall.at[cc, bb, aa, :, others],
@@ -219,8 +219,12 @@
     for one in probs:
         one.second()
     own_h.second()
-    for one in probs:
+    for one in probs[:2]:
         one.relay()
+    for d in range(1, NZ):
+        got(zin.at[NZ - d], zhr.at[d - 1])
+    hall[c, b, a] = jnp.concatenate([hown[c, b, a]] + [zin[d] for d in range(1, NZ)], axis=1)
+    other_h.first()
 
     own = lax.rem(lax.broadcasted_iota(jnp.int32, (RG, NV * RG), 1), RG) == (
         lax.broadcasted_iota(jnp.int32, (RG, NV * RG), 0)
@@ -237,14 +241,14 @@
             targ_ref[n, rows, :] = placed[n * RG : (n + 1) * RG].astype(BF16)
         mass_ref[rows, :] = placed[TILES * RG :]
 
-    for part in range(2):
+    for part, (low, size) in enumerate(PARTS):
         probs[part].last()
         probs[part].finish()
-        pl.loop(part * HALF // RG, (part + 1) * HALF // RG, unroll=2)(place_rows)
-        rows = pl.ds(part * HALF, HALF)
+        pl.loop(low // RG, (low + size) // RG, unroll=2)(place_rows)
+        rows = pl.ds(low, size)
         for d in range(1, NZ):
             to = mod(z + d, NZ)
-            there = pl.ds((NZ - d) * ROWS + part * HALF, HALF)
+            there = pl.ds((NZ - d) * ROWS + low, size)
             for s in range(2):
                 rcopy(
                     targ_ref.at[tile_of(to, s), rows], t_in.at[s, there], ts, tr, at_z(to)
@@ -258,12 +262,10 @@
                 ).start()
 
         if part == 0:
+            probs[2].relay()
             own_h.relay()
-            for d in range(1, NZ):
-                got(zin.at[NZ - d], zhr.at[d - 1])
-            parts = [hown[c, b, a]] + [zin[d] for d in range(1, NZ)]
-            hall[c, b, a] = jnp.concatenate(parts, axis=1)
-            other_h.first()
+        if part == 1:
+            other_h.second()
 
     for s in range(2):
         t_in[s, 0:ROWS] = targ_ref[tile_of(z, s)]
@@ -274,7 +276,6 @@
 
     own_h.last()
     own_h.finish()
-    other_h.second()
     w_copy.wait()
     for i in range(NV // 2):
         yy, xx = i // NS, i % NS
@@ -332,6 +333,8 @@
     counts = jnp.broadcast_to(count_ref[...].astype(F32), (TILE, ROWS)).T
     weighted = jnp.where(counts > me.astype(F32), entries * jnp.log(entries), 0.0)
     shares = jnp.sum((weighted - cross) * scale)
+
+    other_h.relay()
 
     got(stat_in.at[pl.ds(0, NV - 1)], st_r)
     stats = stat_in[...]
@@ -370,7 +373,6 @@
     ghr[me] = ghs[me]
     hall[:, :, :, :, 0:KEPT] = hown[:, :, :, :, 0:KEPT]
 
-    other_h.relay()
     other_h.last()
 
     @pl.loop(1, NV)
@@ -536,7 +538,7 @@
             pltpu.VMEM((NV, 8, TILE), F32),
             pltpu.VMEM((NZ, 8, TILE), F32),
             dma, dma((NZ - 1,)), dma((NZ - 1,)),
-            [dma((11,)), dma((11,))], [dma((11,)), dma((11,))], [dma((11,)), dma((11,))], [dma((11,)), dma((11,))],
+            [dma((11,)), dma((11,))], [dma((11,)), dma((11,))], [dma((11,)), dma((11,))], [dma((11,)), dma((11,))], [dma((11,)), dma((11,))],
             dma, dma, dma, dma, dma, dma, dma, dma, dma, dma,
             dma, dma, dma((NZ,)), dma, dma, dma, dma, dma((SLOTS,)),
         ],

time: 141 us -> 143 us (1.014)
  the two profiles are of different devices: /device:TPU:1 before, /device:TPU:73 now
where the time goes in v4:
time: 143 us
  Pallas kernels  137 us (96%)
  local copies, waits for them, and re-layouts  5.07 us (4%)
    pallas_call x1, Pallas kernels, shards(): pl.pallas_call(kernel, out_shape=(jax.ShapeDtypeStruct((8, TILE), F32), j...  137 us
    unnamed x2, local copies, waits for them, and re-layouts  3.89 us

profile of v4, /device:TPU:73, one launch (start us, length us, event | category | flops | bytes accessed | tf_op | source)
XLA Modules:
  0.0 142.9 jit_solution(14992698761864198030)
XLA Ops:
  0.6 137.2 %shard_map.76 = (f32[8,128]{1,0:T(8,128)}, bf16[64,448]{1,0:T(8,128)(2,1)}, bf16[256,2432]{1,0:T(8,128)(2,1)}) custom-call(bf16[64,448]{1,0:T(8,128)(2,1)} %bitcast.8, bf16[2048,2432]{1,0:T(8,128)(2,1)} %w_hbm.1, s32[32,448]{1,0:T(8,128)} %bitcast.9, s32[1,448]{1,0:T(1,128)} %bitcast.10, bf16[448,128]{1,0:T(8,128)(2,1)} %bitcast.7), custom_call_target="tpu_custom_call" | custom-call | flops 17850957824 | bytes 9961472 | tf_op jit(solution)/shard_map/pallas_call | solution.py:505
  137.9 1.2 slice.3
  139.1 1.5 %copy.10 = bf16[448,64]{0,1:T(8,128)(2,1)} copy(bf16[448,64]{0,1:T(8,128)(2,1)} %bitcast.6) | data formatting | bytes 114688
  140.5 2.4 %copy.11 = bf16[256,2432]{1,0:T(8,128)(2,1)} copy(bf16[256,2432]{1,0:T(8,128)(2,1)} %get-tuple-element.14) | data formatting | bytes 2490368

commit v5 on v4

--- a/solution.py
+++ b/solution.py
@@ -241,12 +241,16 @@
             targ_ref[n, rows, :] = placed[n * RG : (n + 1) * RG].astype(BF16)
         mass_ref[rows, :] = placed[TILES * RG :]
 
-    for part, (low, size) in enumerate(PARTS):
+    def build_part(part):
+        low, size = PARTS[part]
         probs[part].last()
         probs[part].finish()
         pl.loop(low // RG, (low + size) // RG, unroll=2)(place_rows)
+
+    def send_part(part):
+        low, size = PARTS[part]
         rows = pl.ds(low, size)
-        for d in range(1, NZ):
+        for d in (1, 7, 2, 6, 3, 5, 4):
             to = mod(z + d, NZ)
             there = pl.ds((NZ - d) * ROWS + low, size)
             for s in range(2):
@@ -261,11 +265,14 @@
                     ts2.at[d], tr2, at_z(to),
                 ).start()
 
-        if part == 0:
-            probs[2].relay()
-            own_h.relay()
-        if part == 1:
-            other_h.second()
+    build_part(0)
+    send_part(0)
+    probs[2].relay()
+    own_h.relay()
+    build_part(1)
+    other_h.second()
+    send_part(1)
+    build_part(2)
 
     for s in range(2):
         t_in[s, 0:ROWS] = targ_ref[tile_of(z, s)]
@@ -335,6 +342,7 @@
     shares = jnp.sum((weighted - cross) * scale)
 
     other_h.relay()
+    send_part(2)
 
     got(stat_in.at[pl.ds(0, NV - 1)], st_r)
     stats = stat_in[...]

time: 143 us -> 143 us (level)
  no operation moved by 1% of the time
where the time goes in v5:
time: 143 us
  Pallas kernels  137 us (96%)
  local copies, waits for them, and re-layouts  5.07 us (4%)
    pallas_call x1, Pallas kernels, shards(): pl.pallas_call(kernel, out_shape=(jax.ShapeDtypeStruct((8, TILE), F32), j...  137 us
    unnamed x2, local copies, waits for them, and re-layouts  3.89 us

profile of v5, /device:TPU:73, one launch (start us, length us, event | category | flops | bytes accessed | tf_op | source)
XLA Modules:
  0.0 142.9 jit_solution(9612327137248429659)
XLA Ops:
  0.6 137.2 %shard_map.76 = (f32[8,128]{1,0:T(8,128)}, bf16[64,448]{1,0:T(8,128)(2,1)}, bf16[256,2432]{1,0:T(8,128)(2,1)}) custom-call(bf16[64,448]{1,0:T(8,128)(2,1)} %bitcast.8, bf16[2048,2432]{1,0:T(8,128)(2,1)} %w_hbm.1, s32[32,448]{1,0:T(8,128)} %bitcast.9, s32[1,448]{1,0:T(1,128)} %bitcast.10, bf16[448,128]{1,0:T(8,128)(2,1)} %bitcast.7), custom_call_target="tpu_custom_call" | custom-call | flops 17850957824 | bytes 9961472 | tf_op jit(solution)/shard_map/pallas_call | solution.py:513
  137.9 1.2 slice.3
  139.1 1.5 %copy.10 = bf16[448,64]{0,1:T(8,128)(2,1)} copy(bf16[448,64]{0,1:T(8,128)(2,1)} %bitcast.6) | data formatting | bytes 114688
  140.5 2.4 %copy.11 = bf16[256,2432]{1,0:T(8,128)(2,1)} copy(bf16[256,2432]{1,0:T(8,128)(2,1)} %get-tuple-element.14) | data formatting | bytes 2490368

commit v6 on v5

--- a/solution.py
+++ b/solution.py
@@ -55,7 +55,7 @@
 def kernel(
     ht_ref, w_hbm, tiles_ref, count_ref, probs_ref,
     loss_ref, gh_ref, gw_ref,
-    w_ref, hall, hown, zin, lnf_ref, col_ref, h_ref, pbuf, logit_ref, targ_ref, g_ref, z_ref, mass_ref, ln_ref,
+    w_ref, hall, hown, zin, col_ref, h_ref, pbuf, logit_ref, targ_ref, g_ref, z_ref, mass_ref, ln_ref,
     wt_ref, t_in, grad_ref, gws, stat_out, stat_in, stat_z, ghs, ghr, l1, l2,
     w_sem, zhs, zhr, h_sems, p_sems, q_sems, v_sems, o_sems,
     st_s, st_r, gh_s, gh_r, l1s, l1r, l2s, l2r, sz_s, sz_r, ts, tr, ts2, tr2, ws, wr, ws2, wr2,
@@ -342,7 +342,6 @@
     shares = jnp.sum((weighted - cross) * scale)
 
     other_h.relay()
-    send_part(2)
 
     got(stat_in.at[pl.ds(0, NV - 1)], st_r)
     stats = stat_in[...]
@@ -357,6 +356,7 @@
     stat_z[0] = jnp.concatenate([log_norm, scale_rows[0:4]], axis=0)
     for d in range(1, NZ):
         rcopy(stat_z.at[0], stat_z.at[NZ - d], sz_s, sz_r, at_z(mod(z + d, NZ))).start()
+    send_part(2)
     ln_ref[...] = to_all_lanes(log_norm)
     common = jnp.sum(jnp.where(real, log_norm - scale_rows[4:8], 0.0)) * (1.0 / NV)
     l1[me] = jnp.broadcast_to(shares + common, (8, TILE))
@@ -395,24 +395,27 @@
     def _(d):
         rcopy(l2.at[z], l2.at[z], l2s, l2r, at_z(mod(z + d, NZ))).start()
 
-    got(stat_z.at[pl.ds(0, NZ - 1)], sz_r)
-    lnf_ref[...] = jnp.concatenate(
-        [flat_row(stat_z[d, 0:4])[:, :ROWS] for d in range(NZ)], axis=1
-    )
-    for d in range(NZ):
-        col_ref[d * ROWS : (d + 1) * ROWS, :] = to_all_lanes(stat_z[d, 4:8])
     other_h.finish()
 
     @pl.loop(0, ALL // STEP)
     def _(k):
         lanes = pl.ds(pl.multiple_of(k * STEP, STEP), STEP)
         rows = hall[:, :, :, :, lanes].reshape(D, STEP)
-        part = jnp.dot(wt_ref[...], rows, preferred_element_type=F32)
-        soft = (LOSS_SCALE * jnp.exp(part - lnf_ref[:, lanes])).T
+        part = jnp.dot(wt_ref[...], rows, preferred_element_type=F32).T
         for s in range(SLOTS):
             logit_ref[pl.ds(pl.multiple_of(s * ALL + k * STEP, STEP), STEP), :] = (
-                soft[:, s * TILE : (s + 1) * TILE]
+                part[:, s * TILE : (s + 1) * TILE]
             )
+
+    got(stat_z.at[pl.ds(0, NZ - 1)], sz_r)
+
+    @pl.loop(0, NZ)
+    def _(d):
+        norm = to_all_lanes(stat_z[d, 0:4])
+        col_ref[tile_rows(d), :] = to_all_lanes(stat_z[d, 4:8])
+        for s in range(SLOTS):
+            rows = tile_rows(s * NZ + d)
+            logit_ref[rows, :] = LOSS_SCALE * jnp.exp(logit_ref[rows, :] - norm)
 
     got(t_in.at[pl.ds(0, 2), pl.ds(ROWS, ALL - ROWS)], tr)
 
@@ -524,7 +527,6 @@
             pltpu.VMEM((NC, NS, NS, BLK, ALL), BF16),
             pltpu.VMEM((NC, NS, NS, BLK, ROWS), BF16),
             pltpu.VMEM((NZ, BLK, ROWS), BF16),
-            pltpu.VMEM((1, ALL), F32),
             pltpu.VMEM((ALL, TILE), F32),
             pltpu.VMEM((ROWS, D), BF16),
             pltpu.VMEM((NC, NS, NS, ROWS, TILE), BF16),

time: 143 us -> 144 us (level)
  no operation moved by 1% of the time
where the time goes in v6:
time: 144 us
  Pallas kernels  138 us (96%)
  local copies, waits for them, and re-layouts  5.07 us (4%)
    pallas_call x1, Pallas kernels, shards(): pl.pallas_call(kernel, out_shape=(jax.ShapeDtypeStruct((8, TILE), F32), j...  138 us
    unnamed x2, local copies, waits for them, and re-layouts  3.89 us

profile of v6, /device:TPU:73, one launch (start us, length us, event | category | flops | bytes accessed | tf_op | source)
XLA Modules:
  0.0 143.8 jit_solution(1378500727110896852)
XLA Ops:
  0.6 138.1 %shard_map.76 = (f32[8,128]{1,0:T(8,128)}, bf16[64,448]{1,0:T(8,128)(2,1)}, bf16[256,2432]{1,0:T(8,128)(2,1)}) custom-call(bf16[64,448]{1,0:T(8,128)(2,1)} %bitcast.8, bf16[2048,2432]{1,0:T(8,128)(2,1)} %w_hbm.1, s32[32,448]{1,0:T(8,128)} %bitcast.9, s32[1,448]{1,0:T(1,128)} %bitcast.10, bf16[448,128]{1,0:T(8,128)(2,1)} %bitcast.7), custom_call_target="tpu_custom_call" | custom-call | flops 17850957824 | bytes 9961472 | tf_op jit(solution)/shard_map/pallas_call | solution.py:516
  138.8 1.2 slice.3
  140.0 1.5 %copy.10 = bf16[448,64]{0,1:T(8,128)(2,1)} copy(bf16[448,64]{0,1:T(8,128)(2,1)} %bitcast.6) | data formatting | bytes 114688
  141.4 2.4 %copy.11 = bf16[256,2432]{1,0:T(8,128)(2,1)} copy(bf16[256,2432]{1,0:T(8,128)(2,1)} %get-tuple-element.14) | data formatting | bytes 2490368
